TPU v7x, 32 devices: a whole 2x2x4 slice. The times are simulated.
32 devices in a mesh: section: 4 (over x, core), vocab: 8 (over z, y).
Axes of the slice: x: 2, y: 2, z: 4, core: 2. Of those that a mesh axis runs over, the one named last changes fastest.
Arguments:
- token_grad: bfloat16 [8192, 4608], P('vocab', 'section'), may hold values from -6 to 6
- token_ids: int32 [8192], P('vocab'), may hold values from -1 to 519, as said below
- block_counts: int32 [8, 8], P('vocab'), may hold values from 0 to 2, as said below
- hidden: bfloat16 [2048, 4608], P('section'), may hold values from -6 to 6
- dlogits: bfloat16 [2048, 4160], P('section', 'vocab'), may hold values from -0.125 to 0.125
- master: float32 [4160, 4608], P('vocab', 'section'), may hold values from -0.046875 to 0.046875
- moment1: float32 [4160, 4608], P('vocab', 'section'), may hold values from -4 to 4
- moment2: float32 [4160, 4608], P('vocab', 'section'), may hold values from 0.01 to 1
Outputs:
- new_master: float32 [4160, 4608], P('vocab', 'section')
- new_moment1: float32 [4160, 4608], P('vocab', 'section')
- new_moment2: float32 [4160, 4608], P('vocab', 'section')
- refreshed: bfloat16 [4160, 4608], P('vocab')
Inputs may be any that keep to these rules, and one draw needn't show every extreme that they name: `block_counts`: row j gives, for each owner in order, how many of sender j's 8 blocks belong to it; each row sums to 8 and sender j's blocks come in owner order; one owner gets 2 blocks from every sender. `token_ids`: an id is a row among its block's owner's 520 rows, or -1 for a padding row.
All inputs are finite; a program needn't handle non-finite values.
Results may differ from a plain program's by a relative error of at most 0.005.
Values may be sent and summed in bfloat16 or wider, within the bound.
A program may use at most 128 MiB of HBM per device.

v0:
```python
import jax
import jax.numpy as jnp
from jax import lax
from jax.sharding import PartitionSpec as P

BLOCK = 128


beta_first = 0.9
beta_second = 0.999
learn_rate = 0.01
adam_epsilon = 1e-08
first_fix = 1.0 - 0.9**10
second_fix = 1.0 - 0.999**10


def shards(token_grad, token_ids, block_counts, hidden, dlogits, master, moment1, moment2):
    owners = lax.axis_size("vocab")
    row_total, quarter = token_grad.shape
    block_total = row_total // BLOCK
    capacity = max(1, 2 * block_total // owners)
    slab_rows = master.shape[0]
    counts = block_counts[0]
    starts = jnp.cumsum(counts) - counts
    slot_index = jnp.arange(capacity, dtype=jnp.int32)
    live_slot = slot_index[None, :] < counts[:, None]
    pick_index = jnp.where(live_slot, starts[:, None] + slot_index[None, :], 0)
    grad_blocks = token_grad.reshape(block_total, BLOCK, quarter)
    id_blocks = token_ids.reshape(block_total, BLOCK)
    send_rows = grad_blocks[pick_index.reshape(-1)].reshape(owners, capacity * BLOCK, quarter)
    send_ids = jnp.where(live_slot[:, :, None], id_blocks[pick_index], -1).reshape(
        owners, capacity * BLOCK
    )
    got_rows, got_ids = (
        lax.all_to_all(send_rows, "vocab", split_axis=0, concat_axis=0, tiled=True),
        lax.all_to_all(send_ids, "vocab", split_axis=0, concat_axis=0, tiled=True),
    )
    flat_rows = got_rows.reshape(-1, quarter)
    flat_ids = got_ids.reshape(-1)
    one_hot = (jnp.arange(slab_rows, dtype=jnp.int32)[:, None] == flat_ids[None, :]).astype(
        jnp.bfloat16
    )
    token_sum = jnp.dot(one_hot, flat_rows, preferred_element_type=jnp.float32)
    head_grad = (
        lax.psum_scatter(
            lax.dot_general(
                hidden, dlogits, (((0,), (0,)), ((), ())), preferred_element_type=jnp.float32
            ).astype(jnp.bfloat16),
            "section",
            scatter_dimension=0,
            tiled=True,
        )
        .astype(jnp.float32)
        .T
    )
    gradient = token_sum + head_grad
    new_moment1 = beta_first * moment1 + (1.0 - beta_first) * gradient
    new_moment2 = beta_second * moment2 + (1.0 - beta_second) * gradient * gradient
    new_master = master - learn_rate * (new_moment1 / first_fix) / (
        jnp.sqrt(new_moment2 / second_fix) + adam_epsilon
    )
    refreshed = lax.all_gather(new_master.astype(jnp.bfloat16), "section", axis=1, tiled=True)
    return (new_master, new_moment1, new_moment2, refreshed)


def solution(mesh):
    placed = (
        P("vocab", "section"),
        P("vocab"),
        P("vocab", None),
        P("section", None),
        P("section", "vocab"),
        P("vocab", "section"),
        P("vocab", "section"),
        P("vocab", "section"),
    )
    return jax.shard_map(
        shards,
        mesh=mesh,
        in_specs=placed,
        out_specs=(
            P("vocab", "section"),
            P("vocab", "section"),
            P("vocab", "section"),
            P("vocab", None),
        ),
        check_vma=False,
    )
```

profile of v0, /device:TPU:1, one launch (start us, length us, event | category | flops | bytes accessed | tf_op | source)
XLA Modules:
  0.0 205.6 jit_solution(4978834905560198256)
XLA Ops:
  7.2 0.0 copy-start
  7.2 0.0 reduce-scatter.4.cloned.1.call-start
  7.2 7.5 %convolution_convert_fusion = bf16[4608,520]{0,1:T(8,128)(2,1)} fusion(bf16[512,4608]{1,0:T(8,128)(2,1)} %param.11, bf16[512,520]{0,1:T(8,128)(2,1)} %param.12), kind=kOutput, calls=%fused_computation.2 | convolution fusion | flops 2456064000 | bytes 10043392 | tf_op jit(solution)/shard_map/dot_general | solution.py:46
  14.7 8.1 %copy.12 = bf16[4608,520]{1,0:T(8,128)(2,1)} copy(bf16[4608,520]{0,1:T(8,128)(2,1)} %convolution_convert_fusion) | data formatting | bytes 9584640
  22.8 0.0 copy-start.2
  22.8 0.0 copy-start.1
  22.8 0.0 reduce-scatter.4.cloned.1.call-update
  22.8 0.6 copy-done.2
  23.4 0.2 reduce-window.8
  23.6 0.1 compare_select_fusion
  23.7 0.1 reshape.235
  23.8 0.0 copy-done.1
  23.8 0.6 gather_fusion
  24.4 0.1 iota_compare_fusion.5
  24.4 0.7 broadcast_select_fusion
  25.1 6.4 %all-to-all-start = ((s32[8,1,256]{2,1,0:T(1,128)}), s32[8,1,256]{2,1,0:T(1,128)S(1)}, u32[]{:S(2)}, u32[]{:S(2)}) async-start(s32[8,1,256]{2,1,0:T(1,128)} %bitcast.5), calls=%async_computation | async-start | bytes 16384 | tf_op jit(solution)/shard_map/all_to_all | solution.py:36
  31.5 0.1 add_select_fusion
  31.6 0.1 select_n.64
  31.7 0.0 copy-done
  31.7 4.0 %gather_fusion.1 = bf16[16,128,1152]{2,1,0:T(8,128)(2,1)} fusion(bf16[8,128,1152]{2,1,0:T(8,128)(2,1)S(1)} %bitcast.22, s32[1024]{0:T(1024)S(1)} %pad_clamp_fusion), kind=kCustom, calls=%fused_computation.1 | custom fusion | bytes 9437248 | tf_op jit(solution)/shard_map/gather | solution.py:30
  35.7 1.2 all-to-all-done
  36.9 4.6 %all-to-all-start.1 = ((bf16[8,256,1152]{2,1,0:T(8,128)(2,1)}), bf16[8,256,1152]{2,1,0:T(8,128)(2,1)}, u32[]{:S(2)}, u32[]{:S(2)}) async-start(bf16[8,256,1152]{2,1,0:T(8,128)(2,1)} %bitcast.23), calls=%async_computation.1 | async-start | bytes 9437184 | tf_op jit(solution)/shard_map/all_to_all | solution.py:35
  41.5 0.0 all-gather.2.cloned.1.call-start
  41.5 39.2 %reduce-scatter.4.cloned.1.call-done = bf16[1152,520]{1,0:T(8,128)(2,1)} async-done(((bf16[4608,520]{1,0:T(8,128)(2,1)}), bf16[1152,520]{1,0:T(8,128)(2,1)}) %reduce-scatter.4.cloned.1.call-update) | async-done | bytes 1198096
  80.8 2.6 %copy.13 = bf16[1152,520]{0,1:T(8,128)(2,1)} copy(bf16[1152,520]{1,0:T(8,128)(2,1)} %reduce-scatter.4.cloned.1.call-done) | data formatting | bytes 2396160
  83.3 60.5 %all-to-all-done.1 = bf16[8,256,1152]{2,1,0:T(8,128)(2,1)} async-done(((bf16[8,256,1152]{2,1,0:T(8,128)(2,1)}), bf16[8,256,1152]{2,1,0:T(8,128)(2,1)}, u32[]{:S(2)}, u32[]{:S(2)}) %all-to-all-start.1) | async-done | bytes 4718624 | tf_op jit(solution)/shard_map/all_to_all | solution.py:35
  143.9 10.2 %fusion.5 = (bf16[520,1152]{1,0:T(8,128)(2,1)}, f32[520,1152]{1,0:T(8,128)}, f32[520,1152]{1,0:T(8,128)}, f32[520,1152]{1,0:T(8,128)}) fusion(f32[520,1152]{1,0:T(8,128)} %param.13, f32[520,1152]{1,0:T(8,128)} %param.14, f32[520,1152]{1,0:T(8,128)} %param.15, bf16[1152,520]{0,1:T(8,128)(2,1)} %copy.13, bf16[2048,1152]{1,0:T(8,128)(2,1)} %bitcast.10, ...), kind=kOutput, calls=%fused_computation.21 | convolution fusion | flops 2463718400 | bytes 21499904 | tf_op jit(solution)/shard_map/dot_general | solution.py:43
  154.1 0.0 all-gather.2.cloned.1.call-update
  154.1 39.8 %all-gather.2.cloned.1.call-done = bf16[520,4608]{1,0:T(8,128)(2,1)} async-done(((bf16[520,1152]{1,0:T(8,128)(2,1)}), bf16[520,4608]{1,0:T(8,128)(2,1)}) %all-gather.2.cloned.1.call-update) | async-done | bytes 4792336 | tf_op jit(solution)/shard_map/all_gather | solution.py:62
  193.9 4.9 %copy.15 = bf16[520,4608]{1,0:T(8,128)(2,1)} copy(bf16[520,4608]{1,0:T(8,128)(2,1)} %all-gather.2.cloned.1.call-done) | data formatting | bytes 9584640
  (4 shorter events, 0.0 us)
Async XLA Ops:
  7.2 24.5 %copy-start = (bf16[1024,1152]{1,0:T(8,128)(2,1)S(1)}, bf16[1024,1152]{1,0:T(8,128)(2,1)}, u32[]{:S(2)}) copy-start(bf16[1024,1152]{1,0:T(8,128)(2,1)} %param.8) | copy-start | bytes 7077892
  7.2 73.6 %reduce-scatter.4.cloned.1.call-start = ((), (), s32[]{:S(2)}) async-start(), calls=%async_computation.4 | async-start | bytes 7372800
  22.8 0.7 copy-start.2
  22.8 1.0 copy-start.1
  25.1 11.7 %all-to-all-start = ((s32[8,1,256]{2,1,0:T(1,128)}), s32[8,1,256]{2,1,0:T(1,128)S(1)}, u32[]{:S(2)}, u32[]{:S(2)}) async-start(s32[8,1,256]{2,1,0:T(1,128)} %bitcast.5), calls=%async_computation | async-start | bytes 16384 | tf_op jit(solution)/shard_map/all_to_all | solution.py:36
  36.9 107.0 %all-to-all-start.1 = ((bf16[8,256,1152]{2,1,0:T(8,128)(2,1)}), bf16[8,256,1152]{2,1,0:T(8,128)(2,1)}, u32[]{:S(2)}, u32[]{:S(2)}) async-start(bf16[8,256,1152]{2,1,0:T(8,128)(2,1)} %bitcast.23), calls=%async_computation.1 | async-start | bytes 9437184 | tf_op jit(solution)/shard_map/all_to_all | solution.py:35
  41.5 152.4 %all-gather.2.cloned.1.call-start = ((), (), s32[]{:S(2)}) async-start(), calls=%async_computation.3 | async-start | bytes 5990400 | tf_op jit(solution)/shard_map/all_gather | solution.py:62
Sparse Core Ops, SparseCore 0:
  22.9 57.7 reduce-scatter.3
  154.2 39.6 all-gather.1
where the time goes:
time: 206 us
  waiting for transfers between devices  141 us (68%)
  local copies, waits for them, and re-layouts  20.9 us (10%)
  matrix products  17.7 us (9%)
  between operations  14.1 us (7%)
  starting transfers between devices  11.1 us (5%)
    all_to_all x1, waiting for transfers between devices, shards(): lax.all_to_all(send_rows, 'vocab', split_axis=0, concat_axis=0, tiled=True)  60.5 us
    all_gather x1, waiting for transfers between devices, shards(): lax.all_gather(new_master.astype(jnp.bfloat16), 'section', axis=1, tiled=...  39.8 us
    unnamed x3, waiting for transfers between devices  39.3 us
    unnamed x9, local copies, waits for them, and re-layouts  16.2 us
    dot_general x1, matrix products, shards(): token_sum = jnp.dot(one_hot, flat_rows, preferred_element_type=jnp.float32)  10.2 us
    dot_general x1, matrix products, shards(): lax.dot_general(hidden, dlogits, (((0,), (0,)), ((), ())), preferred_elem...  7.47 us
    all_to_all x1, starting transfers between devices, shards(): lax.all_to_all(send_ids, 'vocab', split_axis=0, concat_axis=0, tiled=True)  6.38 us
    all_to_all x1, starting transfers between devices, shards(): lax.all_to_all(send_rows, 'vocab', split_axis=0, concat_axis=0, tiled=True)  4.6 us
  transfers between devices with their start and end apart: 4, of which 4 were waited for; matrix products, arithmetic and copies ran while one was open for 4% of the time, Pallas kernels for 0%

commit v1 on v0

v1 whole, which is shorter than its diff:
```python
import functools

import jax
import jax.numpy as jnp
from jax import lax
from jax.experimental import pallas as pl
from jax.experimental.pallas import tpu as pltpu
from jax.sharding import PartitionSpec as P

BLOCK = 128
LANES = 128
MESH = pl.DeviceIdType.MESH


beta_first = 0.9
beta_second = 0.999
learn_rate = 0.01
adam_epsilon = 1e-08
first_fix = 1.0 - 0.9**10
second_fix = 1.0 - 0.999**10


def kernel(
    owners, sections, capacity,
    counts_ref, ids_ref, grad_hbm, hidden_hbm, dlogits_hbm, master_hbm, moment1_hbm, moment2_hbm,
    master_out, moment1_out, moment2_out, refreshed_out,
    starts, grad, hidden, dlogits, master, moment1, moment2,
    id_send, id_got, row_send, row_got, one_hot, part, part_got, own_part, fresh, fresh_got,
    load_sem, store_sem, id_send_sem, id_recv_sem, row_send_sem, row_recv_sem,
    part_send_sem, part_recv_sem, fresh_send_sem, fresh_recv_sem,
):
    me = lax.axis_index("vocab")
    here = lax.axis_index("section")
    quarter = master.shape[1]
    chunks = quarter // LANES
    slab_rows = master.shape[0]

    loads = [
        pltpu.make_async_copy(source, target, load_sem.at[i])
        for i, (source, target) in enumerate(
            [
                (grad_hbm, grad),
                (dlogits_hbm, dlogits),
                (hidden_hbm, hidden),
                (master_hbm, master),
                (moment1_hbm, moment1),
                (moment2_hbm, moment2),
            ]
        )
    ]
    for load in loads:
        load.start()

    barrier = pltpu.get_barrier_semaphore()

    @pl.loop(1, owners)
    def _(d):
        pl.semaphore_signal(
            barrier, inc=1, device_id={"vocab": lax.rem(me + d, owners)}, device_id_type=MESH
        )

    @pl.loop(1, sections)
    def _(e):
        pl.semaphore_signal(
            barrier, inc=1, device_id={"section": lax.rem(here + e, sections)}, device_id_type=MESH
        )

    def add_start(o, total):
        starts[o] = total
        return total + counts_ref[0, o]

    lax.fori_loop(0, owners, add_start, jnp.int32(0))

    def pick(owner, slot):
        live = slot < counts_ref[0, owner]
        return live, jnp.where(live, starts[owner] + slot, 0)

    def fill_ids(owner, target):
        target[...] = jnp.full((8, BLOCK), -1, jnp.int32)
        for slot in range(capacity):
            live, block = pick(owner, slot)
            target[slot : slot + 1, :] = jnp.where(live, ids_ref[pl.ds(block, 1), :], -1)

    pl.semaphore_wait(barrier, owners - 1 + sections - 1)

    def id_copy(d):
        return pltpu.make_async_remote_copy(
            src_ref=id_send.at[d - 1],
            dst_ref=id_got.at[d - 1],
            send_sem=id_send_sem,
            recv_sem=id_recv_sem,
            device_id={"vocab": lax.rem(me + d, owners)},
            device_id_type=MESH,
        )

    @pl.loop(1, owners)
    def _(d):
        fill_ids(lax.rem(me + d, owners), id_send.at[d - 1])
        id_copy(d).start()

    fill_ids(me, id_got.at[owners - 1])

    loads[0].wait()

    def fill_rows(owner, c, target):
        for slot in range(capacity):
            _, block = pick(owner, slot)
            target[slot * BLOCK : (slot + 1) * BLOCK, :] = grad[
                block, :, pl.ds(pl.multiple_of(c * LANES, LANES), LANES)
            ]

    @pl.loop(0, chunks)
    def _(c):
        @pl.loop(1, owners)
        def _(d):
            owner = lax.rem(me + d, owners)
            fill_rows(owner, c, row_send.at[c, d - 1])
            pltpu.make_async_remote_copy(
                src_ref=row_send.at[c, d - 1],
                dst_ref=row_got.at[c, d - 1],
                send_sem=row_send_sem.at[c],
                recv_sem=row_recv_sem.at[c],
                device_id={"vocab": owner},
                device_id_type=MESH,
            ).start()

        fill_rows(me, c, row_got.at[c, owners - 1])

    loads[1].wait()
    loads[2].wait()

    def head_part(section, c):
        at = pl.multiple_of(section * quarter + c * LANES, LANES)
        return jnp.dot(
            dlogits[...], hidden[:, pl.ds(at, LANES)], preferred_element_type=jnp.float32
        )

    @pl.loop(0, chunks)
    def _(c):
        @pl.loop(1, sections)
        def _(e):
            section = lax.rem(here + e, sections)
            part[c, e - 1] = head_part(section, c).astype(jnp.bfloat16)
            pltpu.make_async_remote_copy(
                src_ref=part.at[c, e - 1],
                dst_ref=part_got.at[c, e - 1],
                send_sem=part_send_sem.at[c],
                recv_sem=part_recv_sem.at[c],
                device_id={"section": section},
                device_id_type=MESH,
            ).start()

        own_part[c] = head_part(here, c)

    arrived = id_got.at[pl.ds(0, owners - 1)]
    pltpu.make_async_copy(arrived, arrived, id_recv_sem).wait()

    @pl.loop(0, owners)
    def _(s):
        for slot in range(capacity):
            ids = id_got[s, slot : slot + 1, :]
            rows = lax.broadcasted_iota(jnp.int32, (slab_rows, BLOCK), 0)
            at = pl.multiple_of((s * capacity + slot) * BLOCK, BLOCK)
            one_hot[:, pl.ds(at, BLOCK)] = jnp.where(rows == ids, 1.0, 0.0).astype(jnp.bfloat16)

    for load in loads[3:]:
        load.wait()

    @pl.loop(0, chunks)
    def _(c):
        cols = pl.ds(pl.multiple_of(c * LANES, LANES), LANES)
        rows_in = row_got.at[c, pl.ds(0, owners - 1)]
        pltpu.make_async_copy(rows_in, rows_in, row_recv_sem.at[c]).wait()
        parts_in = part_got.at[c]
        pltpu.make_async_copy(parts_in, parts_in, part_recv_sem.at[c]).wait()
        gradient = jnp.dot(
            one_hot[...],
            row_got[c].reshape(owners * capacity * BLOCK, LANES),
            preferred_element_type=jnp.float32,
        )
        head = own_part[c]
        for e in range(sections - 1):
            head = head + part_got[c, e].astype(jnp.float32)
        gradient = gradient + head
        new_moment1 = beta_first * moment1[:, cols] + (1.0 - beta_first) * gradient
        new_moment2 = beta_second * moment2[:, cols] + (1.0 - beta_second) * gradient * gradient
        new_master = master[:, cols] - learn_rate * (new_moment1 / first_fix) / (
            jnp.sqrt(new_moment2 / second_fix) + adam_epsilon
        )
        fresh[c] = new_master.astype(jnp.bfloat16)

        @pl.loop(1, sections)
        def _(e):
            pltpu.make_async_remote_copy(
                src_ref=fresh.at[c],
                dst_ref=fresh_got.at[c, e - 1],
                send_sem=fresh_send_sem.at[c],
                recv_sem=fresh_recv_sem.at[c],
                device_id={"section": lax.rem(here + e, sections)},
                device_id_type=MESH,
            ).start()

        moment1[:, cols] = new_moment1
        moment2[:, cols] = new_moment2
        master[:, cols] = new_master
        pltpu.make_async_copy(master.at[:, cols], master_out.at[:, cols], store_sem.at[0]).start()
        pltpu.make_async_copy(moment1.at[:, cols], moment1_out.at[:, cols], store_sem.at[1]).start()
        pltpu.make_async_copy(moment2.at[:, cols], moment2_out.at[:, cols], store_sem.at[2]).start()
        at = pl.multiple_of(here * quarter + c * LANES, LANES)
        pltpu.make_async_copy(
            fresh.at[c], refreshed_out.at[:, pl.ds(at, LANES)], store_sem.at[3]
        ).start()

    @pl.loop(0, chunks)
    def _(c):
        fresh_in = fresh_got.at[c]
        pltpu.make_async_copy(fresh_in, fresh_in, fresh_recv_sem.at[c]).wait()

        @pl.loop(1, sections)
        def _(e):
            source = lax.rem(here + sections - e, sections)
            at = pl.multiple_of(source * quarter + c * LANES, LANES)
            pltpu.make_async_copy(
                fresh_got.at[c, e - 1], refreshed_out.at[:, pl.ds(at, LANES)], store_sem.at[3]
            ).start()

    pltpu.make_async_copy(id_send, id_send, id_send_sem).wait()

    @pl.loop(0, chunks)
    def _(c):
        pltpu.make_async_copy(row_send.at[c], row_send.at[c], row_send_sem.at[c]).wait()
        pltpu.make_async_copy(part.at[c], part.at[c], part_send_sem.at[c]).wait()
        pltpu.make_async_copy(fresh_got.at[c], fresh_got.at[c], fresh_send_sem.at[c]).wait()

    pltpu.make_async_copy(master, master_out, store_sem.at[0]).wait()
    pltpu.make_async_copy(moment1, moment1_out, store_sem.at[1]).wait()
    pltpu.make_async_copy(moment2, moment2_out, store_sem.at[2]).wait()
    pltpu.make_async_copy(refreshed_out, refreshed_out, store_sem.at[3]).wait()


def shards(token_grad, token_ids, block_counts, hidden, dlogits, master, moment1, moment2):
    owners = lax.axis_size("vocab")
    sections = lax.axis_size("section")
    row_total, quarter = token_grad.shape
    block_total = row_total // BLOCK
    capacity = max(1, 2 * block_total // owners)
    slab_rows = master.shape[0]
    tokens, width = hidden.shape
    chunks = quarter // LANES
    slots = capacity * BLOCK
    f32, bf16 = jnp.float32, jnp.bfloat16
    hbm = pl.BlockSpec(memory_space=pl.ANY)
    dma = pltpu.SemaphoreType.DMA
    slab = (slab_rows, quarter)
    return pl.pallas_call(
        functools.partial(kernel, owners, sections, capacity),
        out_shape=(
            jax.ShapeDtypeStruct(slab, f32),
            jax.ShapeDtypeStruct(slab, f32),
            jax.ShapeDtypeStruct(slab, f32),
            jax.ShapeDtypeStruct((slab_rows, width), bf16),
        ),
        in_specs=[
            pl.BlockSpec(memory_space=pltpu.SMEM),
            pl.BlockSpec(memory_space=pltpu.VMEM),
            hbm, hbm, hbm, hbm, hbm, hbm,
        ],
        out_specs=(hbm, hbm, hbm, hbm),
        scratch_shapes=[
            pltpu.SMEM((owners,), jnp.int32),
            pltpu.VMEM((block_total, BLOCK, quarter), bf16),
            pltpu.VMEM((tokens, width), bf16),
            pltpu.VMEM((slab_rows, tokens), bf16),
            pltpu.VMEM(slab, f32),
            pltpu.VMEM(slab, f32),
            pltpu.VMEM(slab, f32),
            pltpu.VMEM((owners - 1, 8, BLOCK), jnp.int32),
            pltpu.VMEM((owners, 8, BLOCK), jnp.int32),
            pltpu.VMEM((chunks, owners - 1, slots, LANES), bf16),
            pltpu.VMEM((chunks, owners, slots, LANES), bf16),
            pltpu.VMEM((slab_rows, owners * slots), bf16),
            pltpu.VMEM((chunks, sections - 1, slab_rows, LANES), bf16),
            pltpu.VMEM((chunks, sections - 1, slab_rows, LANES), bf16),
            pltpu.VMEM((chunks, slab_rows, LANES), f32),
            pltpu.VMEM((chunks, slab_rows, LANES), bf16),
            pltpu.VMEM((chunks, sections - 1, slab_rows, LANES), bf16),
            dma((6,)),
            dma((4,)),
            dma,
            dma,
            dma((chunks,)),
            dma((chunks,)),
            dma((chunks,)),
            dma((chunks,)),
            dma((chunks,)),
            dma((chunks,)),
        ],
        compiler_params=pltpu.CompilerParams(
            collective_id=0, has_side_effects=True, vmem_limit_bytes=58 * 1024 * 1024
        ),
    )(
        block_counts,
        token_ids.reshape(block_total, BLOCK),
        token_grad.reshape(block_total, BLOCK, quarter),
        hidden,
        dlogits.T,
        master,
        moment1,
        moment2,
    )


def solution(mesh):
    placed = (
        P("vocab", "section"),
        P("vocab"),
        P("vocab", None),
        P("section", None),
        P("section", "vocab"),
        P("vocab", "section"),
        P("vocab", "section"),
        P("vocab", "section"),
    )
    return jax.shard_map(
        shards,
        mesh=mesh,
        in_specs=placed,
        out_specs=(
            P("vocab", "section"),
            P("vocab", "section"),
            P("vocab", "section"),
            P("vocab", None),
        ),
        check_vma=False,
    )
```

time: 206 us -> 129 us (0.63)
  waiting for transfers between devices: 141 us -> 0 us
  Pallas kernels: 0 us -> 116 us
  matrix products: 17.7 us -> 0 us
  between operations: 14.1 us -> 0.65 us
  starting transfers between devices: 11.1 us -> 0 us
  local copies, waits for them, and re-layouts: 20.9 us -> 10.4 us
    pallas_call x0 -> x1, Pallas kernels: none -> 116 us  [shards(): pl.pallas_call(functools.partial(kernel, owners, sections, capacity), out...]
    all_to_all x2 -> x0, waiting for transfers between devices: 61.7 us -> none  [the longest x1 60.5 us: shards(): lax.all_to_all(send_rows, 'vocab', split_axis=0, concat_axis=0, tiled=True)]
    all_gather x1 -> x0, waiting for transfers between devices: 39.8 us -> none  [shards(): lax.all_gather(new_master.astype(jnp.bfloat16), 'section', axis=1, tiled=...]
    unnamed x3 -> x0, waiting for transfers between devices: 39.3 us -> none
    dot_general x2 -> x0, matrix products: 17.7 us -> none  [the longest x1 10.2 us: shards(): token_sum = jnp.dot(one_hot, flat_rows, preferred_element_type=jnp.float32)]
    all_to_all x2 -> x0, starting transfers between devices: 11 us -> none  [the longest x1 6.38 us: shards(): lax.all_to_all(send_ids, 'vocab', split_axis=0, concat_axis=0, tiled=True)]
    unnamed x9 -> x10, local copies, waits for them, and re-layouts: 16.2 us -> 10.4 us
    gather x2 -> x0, local copies, waits for them, and re-layouts: 4.6 us -> none  [the longest x1 4.03 us: shards(): grad_blocks[pick_index.reshape(-1)]]
  transfers between devices with their start and end apart: 4 -> 0, of which waited for: 4 -> 0; matrix products, arithmetic and copies ran while one was open for 4% -> 0% of each run, Pallas kernels for 0% -> 0%
where the time goes in v1:
time: 129 us; the launch traced here: 127 us
  Pallas kernels  116 us (90%)
  local copies, waits for them, and re-layouts  10.4 us (8%)
    pallas_call x1, Pallas kernels, shards(): pl.pallas_call(functools.partial(kernel, owners, sections, capacity), out...  116 us
    unnamed x10, local copies, waits for them, and re-layouts  10.4 us

profile of v1, /device:TPU:1, one launch (start us, length us, event | category | flops | bytes accessed | tf_op | source)
XLA Modules:
  0.0 126.6 jit_solution(15445901302236758209)
XLA Ops:
  0.6 115.5 %shard_map.111 = (f32[520,1152]{1,0:T(8,128)}, f32[520,1152]{1,0:T(8,128)}, f32[520,1152]{1,0:T(8,128)}, bf16[520,4608]{1,0:T(8,128)(2,1)}) custom-call(s32[1,8]{1,0:T(1,128)} %counts_ref.1, s32[8,128]{1,0:T(8,128)} %bitcast.7, bf16[8,128,1152]{2,1,0:T(8,128)(2,1)} %bitcast.5, bf16[512,4608]{1,0:T(8,128)(2,1)} %hidden_hbm.1, bf16[520,512]{1,0:T(8,128)(2,1)} %bitcast.6, ...), custom_call_target="tpu_custom_call" | custom-call | tf_op jit(solution)/shard_map/pallas_call | solution.py:255
  116.2 0.0 slice-start
  116.2 3.4 %copy.16 = f32[520,1152]{1,0:T(8,128)} copy(f32[520,1152]{1,0:T(8,128)} %get-tuple-element.8) | data formatting | bytes 4792320
  119.6 0.0 copy-start
  119.6 0.0 slice-start.1
  119.6 3.4 %copy.17 = f32[520,1152]{1,0:T(8,128)} copy(f32[520,1152]{1,0:T(8,128)} %get-tuple-element.9) | data formatting | bytes 4792320
  123.0 0.0 copy-done
  123.0 1.4 %copy.18 = f32[520,1152]{1,0:T(8,128)} copy(f32[520,1152]{1,0:T(8,128)S(1)} %copy-done) | data formatting | bytes 4792320
  124.4 0.0 slice-done
  124.4 0.0 slice-done.1
  124.4 2.2 %copy.19 = bf16[520,4608]{1,0:T(8,128)(2,1)} copy(bf16[520,4608]{1,0:T(8,128)(2,1)S(1)} %bitcast.4) | data formatting | bytes 9584640
  (1 shorter events, 0.0 us)
Async XLA Ops:
  116.2 8.2 %slice-start = ((s8[4792320]{0:T(1024)(128)(4,1)}), s8[4194304]{0:T(1024)(128)(4,1)S(1)}, s32[]{:S(2)}) async-start(s8[4792320]{0:T(1024)(128)(4,1)} %bitcast.3), calls=%async_computation | async-start | bytes 8388608
  119.6 3.4 %copy-start = (f32[520,1152]{1,0:T(8,128)S(1)}, f32[520,1152]{1,0:T(8,128)}, u32[]{:S(2)}) copy-start(f32[520,1152]{1,0:T(8,128)} %get-tuple-element.10) | copy-start | bytes 7188484
  119.6 4.8 %slice-start.1 = ((s8[4792320]{0:T(1024)(128)(4,1)}), s8[598016]{0:T(1024)(128)(4,1)S(1)}, s32[]{:S(2)}) async-start(s8[4792320]{0:T(1024)(128)(4,1)} %bitcast.3), calls=%async_computation.1 | async-start | bytes 1196032

commit v2 on v1

--- a/solution.py
+++ b/solution.py
@@ -20,7 +20,7 @@
 second_fix = 1.0 - 0.999**10
 
 
-def kernel(
+def direct_kernel(
     owners, sections, capacity,
     counts_ref, ids_ref, grad_hbm, hidden_hbm, dlogits_hbm, master_hbm, moment1_hbm, moment2_hbm,
     master_out, moment1_out, moment2_out, refreshed_out,
@@ -238,7 +238,7 @@
     pltpu.make_async_copy(refreshed_out, refreshed_out, store_sem.at[3]).wait()
 
 
-def shards(token_grad, token_ids, block_counts, hidden, dlogits, master, moment1, moment2):
+def direct_shards(token_grad, token_ids, block_counts, hidden, dlogits, master, moment1, moment2):
     owners = lax.axis_size("vocab")
     sections = lax.axis_size("section")
     row_total, quarter = token_grad.shape
@@ -253,7 +253,7 @@
     dma = pltpu.SemaphoreType.DMA
     slab = (slab_rows, quarter)
     return pl.pallas_call(
-        functools.partial(kernel, owners, sections, capacity),
+        functools.partial(direct_kernel, owners, sections, capacity),
         out_shape=(
             jax.ShapeDtypeStruct(slab, f32),
             jax.ShapeDtypeStruct(slab, f32),
@@ -310,6 +310,426 @@
     )
 
 
+def relay_kernel(
+    capacity,
+    counts_ref, ids_ref, grad_hbm, hidden_hbm, dlogits_hbm, master_hbm, moment1_hbm, moment2_hbm,
+    master_out, moment1_out, moment2_out, refreshed_out,
+    starts, grad, hidden, dlogits, master, moment1, moment2,
+    slab_ids, id_send, id_got, slot_send, slot_got, raw_got,
+    own_hot, raw_hot, slot_hot, far_hot, total, far_keep, relay_send, relay_got, far_send, far_got,
+    pair_send, pair_got, cross_send, cross_got, own_part, fresh, fresh_got,
+    load_sem, store_sem, id_sems, slot_sems, raw_sems, relay_sems, far_sems,
+    pair_sems, cross_sems, side_sems, over_sems, forward_sems,
+):
+    owners = counts_ref.shape[1]
+    me = lax.axis_index("vocab")
+    here = lax.axis_index("section")
+    z, y = me // 2, lax.rem(me, 2)
+    mate_z = z + 1 - 2 * lax.rem(z, 2)
+    mate = mate_z * 2 + y
+    level = z * 2 + 1 - y
+    corner = mate_z * 2 + 1 - y
+    near = (mate, level, corner)
+    inner = jnp.logical_or(z == 1, z == 2)
+    outer = jnp.logical_not(inner)
+    far_inner_z = 3 - z
+    far_outer_z = lax.rem(z + 2, 4)
+    far = (
+        far_inner_z * 2 + 1 - y,
+        far_outer_z * 2 + 1 - y,
+        far_inner_z * 2 + y,
+        far_outer_z * 2 + y,
+    )
+    sections = 4
+    sibling = here + 1 - 2 * lax.rem(here, 2)
+    across = lax.rem(here + 2, sections)
+    other = lax.rem(sibling + 2, sections)
+    slab_rows, quarter = master.shape
+    blocks = grad.shape[0]
+    chunks = quarter // LANES
+    slots = capacity * BLOCK
+
+    loads = [
+        pltpu.make_async_copy(source, target, load_sem.at[i])
+        for i, (source, target) in enumerate(
+            [
+                (grad_hbm, grad),
+                (dlogits_hbm, dlogits),
+                (hidden_hbm, hidden),
+                (master_hbm, master),
+                (moment1_hbm, moment1),
+                (moment2_hbm, moment2),
+            ]
+        )
+    ]
+    for load in loads:
+        load.start()
+
+    barrier = pltpu.get_barrier_semaphore()
+
+    @pl.loop(1, owners)
+    def _(d):
+        pl.semaphore_signal(
+            barrier, inc=1, device_id={"vocab": lax.rem(me + d, owners)}, device_id_type=MESH
+        )
+
+    @pl.loop(1, sections)
+    def _(e):
+        pl.semaphore_signal(
+            barrier, inc=1, device_id={"section": lax.rem(here + e, sections)}, device_id_type=MESH
+        )
+
+    def send(source, target, sems, where, c=None):
+        return pltpu.make_async_remote_copy(
+            src_ref=source,
+            dst_ref=target,
+            send_sem=sems.at[0] if c is None else sems.at[0, c],
+            recv_sem=sems.at[1] if c is None else sems.at[1, c],
+            device_id=where,
+            device_id_type=MESH,
+        ).start()
+
+    def await_bytes(ref, sem):
+        pltpu.make_async_copy(ref, ref, sem).wait()
+
+    def add_start(o, so_far):
+        starts[o] = so_far
+        return so_far + counts_ref[0, o]
+
+    lax.fori_loop(0, owners, add_start, jnp.int32(0))
+
+    def pick(owner, slot):
+        live = slot < counts_ref[0, owner]
+        return live, jnp.where(live, starts[owner] + slot, 0)
+
+    for b in range(blocks):
+        owner = lax.fori_loop(
+            0,
+            owners,
+            lambda o, n: n + jnp.where(starts[o] + counts_ref[0, o] <= b, 1, 0),
+            jnp.int32(0),
+        )
+        ids = ids_ref[b : b + 1, :]
+        slab_ids[b : b + 1, :] = jnp.where(ids >= 0, ids + owner * slab_rows, -1)
+
+    for i, owner in enumerate(near):
+        id_send[i, 0:blocks, :] = slab_ids[...]
+        id_send[i, blocks:, :] = jnp.full((8, BLOCK), -1, jnp.int32)
+        for slot in range(capacity):
+            live, block = pick(owner, slot)
+            row = blocks + slot
+            id_send[i, row : row + 1, :] = jnp.where(live, ids_ref[pl.ds(block, 1), :], -1)
+
+    pl.semaphore_wait(barrier, owners - 1 + sections - 1)
+
+    for i, owner in enumerate(near):
+        send(id_send.at[i], id_got.at[i], id_sems, {"vocab": owner})
+
+    loads[0].wait()
+
+    def columns(c):
+        return pl.ds(pl.multiple_of(c * LANES, LANES), LANES)
+
+    def send_slot(i, c):
+        for slot in range(capacity):
+            _, block = pick(near[i], slot)
+            slot_send[c, i, slot * BLOCK : (slot + 1) * BLOCK, :] = grad[block, :, columns(c)]
+        send(slot_send.at[c, i], slot_got.at[c, i], slot_sems, {"vocab": near[i]}, c)
+
+    @pl.loop(0, chunks)
+    def _(c):
+        @pl.when(outer)
+        def _():
+            send(grad.at[:, :, columns(c)], raw_got.at[c], raw_sems, {"vocab": mate}, c)
+
+        @pl.when(inner)
+        def _():
+            send_slot(0, c)
+
+        send_slot(1, c)
+        send_slot(2, c)
+
+    loads[1].wait()
+    loads[2].wait()
+
+    def head_part(section, c):
+        at = pl.multiple_of(section * quarter + c * LANES, LANES)
+        return jnp.dot(
+            dlogits[...], hidden[:, pl.ds(at, LANES)], preferred_element_type=jnp.float32
+        )
+
+    @pl.loop(0, chunks)
+    def _(c):
+        pair_send[c, 0] = head_part(sibling, c).astype(jnp.bfloat16)
+        pair_send[c, 1] = head_part(other, c).astype(jnp.bfloat16)
+        send(pair_send.at[c], pair_got.at[c], pair_sems, {"section": sibling}, c)
+
+    def one_hot(ids, base):
+        rows = lax.broadcasted_iota(jnp.int32, (slab_rows, BLOCK), 0) + base
+        return jnp.where(rows == ids, 1.0, 0.0).astype(jnp.bfloat16)
+
+    await_bytes(id_got, id_sems.at[1])
+
+    def block_lanes(b):
+        return pl.ds(pl.multiple_of(b * BLOCK, BLOCK), BLOCK)
+
+    @pl.when(inner)
+    def _():
+        @pl.loop(0, blocks)
+        def _(b):
+            own_ids = slab_ids[pl.ds(b, 1), :]
+            mate_ids = id_got[0, pl.ds(b, 1), :]
+            raw_hot[:, block_lanes(b)] = one_hot(mate_ids, me * slab_rows)
+            for f in range(4):
+                far_hot[f, :, block_lanes(b)] = one_hot(own_ids, far[f] * slab_rows)
+                far_hot[f, :, block_lanes(blocks + b)] = one_hot(mate_ids, far[f] * slab_rows)
+
+    @pl.loop(0, chunks)
+    def _(c):
+        own_part[c] = head_part(here, c)
+        mine = head_part(across, c)
+        await_bytes(pair_got.at[c], pair_sems.at[1, c])
+        cross_send[c] = (mine + pair_got[c, 1].astype(jnp.float32)).astype(jnp.bfloat16)
+        send(cross_send.at[c], cross_got.at[c], cross_sems, {"section": across}, c)
+
+    @pl.loop(0, blocks)
+    def _(b):
+        own_hot[:, block_lanes(b)] = one_hot(slab_ids[pl.ds(b, 1), :], me * slab_rows)
+
+    for i in range(3):
+        for slot in range(capacity):
+            at = (i * capacity + slot) * BLOCK
+            row = blocks + slot
+            slot_hot[:, at : at + BLOCK] = one_hot(id_got[i, row : row + 1, :], 0)
+
+    for load in loads[3:]:
+        load.wait()
+
+    def dot(a, b):
+        return jnp.dot(a, b, preferred_element_type=jnp.float32)
+
+    def own_rows(c):
+        return grad[:, :, columns(c)].reshape(blocks * BLOCK, LANES)
+
+    def raw_rows(c):
+        return raw_got[c].reshape(blocks * BLOCK, LANES)
+
+    half = blocks * BLOCK
+
+    def far_sum(f, c):
+        return dot(far_hot[f, :, 0:half], own_rows(c)) + dot(far_hot[f, :, half:], raw_rows(c))
+
+    def gather_far(c):
+        await_bytes(raw_got.at[c], raw_sems.at[1, c])
+        for f in range(2):
+            relay_send[c, f] = far_sum(f, c).astype(jnp.bfloat16)
+        send(relay_send.at[c], relay_got.at[c], relay_sems, {"vocab": level}, c)
+        for f in range(2):
+            far_keep[lax.rem(c, 2), f] = far_sum(2 + f, c)
+
+    def send_far(c):
+        await_bytes(relay_got.at[c], relay_sems.at[1, c])
+        for f in range(2):
+            far_send[c, f] = (
+                far_keep[lax.rem(c, 2), f] + relay_got[c, f].astype(jnp.float32)
+            ).astype(jnp.bfloat16)
+            send(far_send.at[c, f], far_got.at[c], far_sems, {"vocab": far[2 + f]}, c)
+
+    def update(c):
+        cols = columns(c)
+        await_bytes(far_got.at[c], far_sems.at[1, c])
+        await_bytes(cross_got.at[c], cross_sems.at[1, c])
+
+        @pl.when(inner)
+        def _():
+            await_bytes(slot_got.at[c, pl.ds(1, 2)], slot_sems.at[1, c])
+            total[...] = (
+                dot(own_hot[...], own_rows(c))
+                + dot(raw_hot[...], raw_rows(c))
+                + dot(slot_hot[:, slots:], slot_got[c, 1:3].reshape(2 * slots, LANES))
+            )
+
+        @pl.when(outer)
+        def _():
+            await_bytes(slot_got.at[c], slot_sems.at[1, c])
+            total[...] = dot(own_hot[...], own_rows(c)) + dot(
+                slot_hot[...], slot_got[c].reshape(3 * slots, LANES)
+            )
+
+        gradient = (
+            total[...]
+            + far_got[c].astype(jnp.float32)
+            + own_part[c]
+            + pair_got[c, 0].astype(jnp.float32)
+            + cross_got[c].astype(jnp.float32)
+        )
+        new_moment1 = beta_first * moment1[:, cols] + (1.0 - beta_first) * gradient
+        new_moment2 = beta_second * moment2[:, cols] + (1.0 - beta_second) * gradient * gradient
+        new_master = master[:, cols] - learn_rate * (new_moment1 / first_fix) / (
+            jnp.sqrt(new_moment2 / second_fix) + adam_epsilon
+        )
+        fresh[c] = new_master.astype(jnp.bfloat16)
+        send(fresh.at[c], fresh_got.at[c, 1], over_sems, {"section": across}, c)
+        send(fresh.at[c], fresh_got.at[c, 0], side_sems, {"section": sibling}, c)
+        moment1[:, cols] = new_moment1
+        moment2[:, cols] = new_moment2
+        master[:, cols] = new_master
+        pltpu.make_async_copy(master.at[:, cols], master_out.at[:, cols], store_sem.at[0]).start()
+        pltpu.make_async_copy(moment1.at[:, cols], moment1_out.at[:, cols], store_sem.at[1]).start()
+        pltpu.make_async_copy(moment2.at[:, cols], moment2_out.at[:, cols], store_sem.at[2]).start()
+        store_fresh(fresh.at[c], here, c)
+
+    def store_fresh(source, section, c):
+        at = pl.multiple_of(section * quarter + c * LANES, LANES)
+        pltpu.make_async_copy(
+            source, refreshed_out.at[:, pl.ds(at, LANES)], store_sem.at[3]
+        ).start()
+
+    def forward(c):
+        await_bytes(fresh_got.at[c, 1], over_sems.at[1, c])
+        send(fresh_got.at[c, 1], fresh_got.at[c, 2], forward_sems, {"section": sibling}, c)
+        store_fresh(fresh_got.at[c, 1], across, c)
+        await_bytes(fresh_got.at[c, 0], side_sems.at[1, c])
+        store_fresh(fresh_got.at[c, 0], sibling, c)
+
+    def finish(c):
+        await_bytes(fresh_got.at[c, 2], forward_sems.at[1, c])
+        store_fresh(fresh_got.at[c, 2], other, c)
+
+    @pl.loop(0, chunks + 6)
+    def _(t):
+        @pl.when(jnp.logical_and(inner, t < chunks))
+        def _():
+            gather_far(t)
+
+        @pl.when(jnp.logical_and(inner, jnp.logical_and(t >= 1, t < chunks + 1)))
+        def _():
+            send_far(t - 1)
+
+        @pl.when(jnp.logical_and(t >= 3, t < chunks + 3))
+        def _():
+            update(t - 3)
+
+        @pl.when(jnp.logical_and(t >= 5, t < chunks + 5))
+        def _():
+            forward(t - 5)
+
+        @pl.when(t >= 6)
+        def _():
+            finish(t - 6)
+
+    await_bytes(id_send, id_sems.at[0])
+
+    @pl.loop(0, chunks)
+    def _(c):
+        @pl.when(outer)
+        def _():
+            await_bytes(raw_got.at[c], raw_sems.at[0, c])
+            await_bytes(slot_send.at[c, pl.ds(1, 2)], slot_sems.at[0, c])
+
+        @pl.when(inner)
+        def _():
+            await_bytes(slot_send.at[c], slot_sems.at[0, c])
+            await_bytes(relay_send.at[c], relay_sems.at[0, c])
+            await_bytes(far_send.at[c], far_sems.at[0, c])
+
+        await_bytes(pair_send.at[c], pair_sems.at[0, c])
+        await_bytes(cross_send.at[c], cross_sems.at[0, c])
+        await_bytes(fresh.at[c], side_sems.at[0, c])
+        await_bytes(fresh.at[c], over_sems.at[0, c])
+        await_bytes(fresh.at[c], forward_sems.at[0, c])
+
+    pltpu.make_async_copy(master, master_out, store_sem.at[0]).wait()
+    pltpu.make_async_copy(moment1, moment1_out, store_sem.at[1]).wait()
+    pltpu.make_async_copy(moment2, moment2_out, store_sem.at[2]).wait()
+    pltpu.make_async_copy(refreshed_out, refreshed_out, store_sem.at[3]).wait()
+
+
+def relay_shards(token_grad, token_ids, block_counts, hidden, dlogits, master, moment1, moment2):
+    owners = lax.axis_size("vocab")
+    row_total, quarter = token_grad.shape
+    blocks = row_total // BLOCK
+    capacity = max(1, 2 * blocks // owners)
+    slab_rows = master.shape[0]
+    tokens, width = hidden.shape
+    chunks = quarter // LANES
+    slots = capacity * BLOCK
+    f32, bf16, i32 = jnp.float32, jnp.bfloat16, jnp.int32
+    hbm = pl.BlockSpec(memory_space=pl.ANY)
+    dma = pltpu.SemaphoreType.DMA
+    slab = (slab_rows, quarter)
+    piece = (slab_rows, LANES)
+    return pl.pallas_call(
+        functools.partial(relay_kernel, capacity),
+        out_shape=(
+            jax.ShapeDtypeStruct(slab, f32),
+            jax.ShapeDtypeStruct(slab, f32),
+            jax.ShapeDtypeStruct(slab, f32),
+            jax.ShapeDtypeStruct((slab_rows, width), bf16),
+        ),
+        in_specs=[
+            pl.BlockSpec(memory_space=pltpu.SMEM),
+            pl.BlockSpec(memory_space=pltpu.VMEM),
+            hbm, hbm, hbm, hbm, hbm, hbm,
+        ],
+        out_specs=(hbm, hbm, hbm, hbm),
+        scratch_shapes=[
+            pltpu.SMEM((owners,), i32),
+            pltpu.VMEM((blocks, BLOCK, quarter), bf16),
+            pltpu.VMEM((tokens, width), bf16),
+            pltpu.VMEM((slab_rows, tokens), bf16),
+            pltpu.VMEM(slab, f32),
+            pltpu.VMEM(slab, f32),
+            pltpu.VMEM(slab, f32),
+            pltpu.VMEM((blocks, BLOCK), i32),
+            pltpu.VMEM((3, blocks + 8, BLOCK), i32),
+            pltpu.VMEM((3, blocks + 8, BLOCK), i32),
+            pltpu.VMEM((chunks, 3, slots, LANES), bf16),
+            pltpu.VMEM((chunks, 3, slots, LANES), bf16),
+            pltpu.VMEM((chunks, blocks, BLOCK, LANES), bf16),
+            pltpu.VMEM((slab_rows, row_total), bf16),
+            pltpu.VMEM((slab_rows, row_total), bf16),
+            pltpu.VMEM((slab_rows, 3 * slots), bf16),
+            pltpu.VMEM((4, slab_rows, 2 * row_total), bf16),
+            pltpu.VMEM(piece, f32),
+            pltpu.VMEM((2, 2) + piece, f32),
+            pltpu.VMEM((chunks, 2) + piece, bf16),
+            pltpu.VMEM((chunks, 2) + piece, bf16),
+            pltpu.VMEM((chunks, 2) + piece, bf16),
+            pltpu.VMEM((chunks,) + piece, bf16),
+            pltpu.VMEM((chunks, 2) + piece, bf16),
+            pltpu.VMEM((chunks, 2) + piece, bf16),
+            pltpu.VMEM((chunks,) + piece, bf16),
+            pltpu.VMEM((chunks,) + piece, bf16),
+            pltpu.VMEM((chunks,) + piece, f32),
+            pltpu.VMEM((chunks,) + piece, bf16),
+            pltpu.VMEM((chunks, 3) + piece, bf16),
+            dma((6,)),
+            dma((4,)),
+            dma((2,)),
+        ]
+        + [dma((2, chunks)) for _ in range(9)],
+        compiler_params=pltpu.CompilerParams(
+            collective_id=1, has_side_effects=True, vmem_limit_bytes=58 * 1024 * 1024
+        ),
+    )(
+        block_counts,
+        token_ids.reshape(blocks, BLOCK),
+        token_grad.reshape(blocks, BLOCK, quarter),
+        hidden,
+        dlogits.T,
+        master,
+        moment1,
+        moment2,
+    )
+
+
+def shards(*arrays):
+    if lax.axis_size("vocab") == 8 and lax.axis_size("section") == 4:
+        return relay_shards(*arrays)
+    return direct_shards(*arrays)
+
+
 def solution(mesh):
     placed = (
         P("vocab", "section"),

time: 129 us -> 115 us (0.89); the launches traced: 127 us -> 115 us
  Pallas kernels: 116 us -> 104 us
    pallas_call x1, Pallas kernels: 116 us -> 104 us  [relay_shards(): pl.pallas_call(functools.partial(relay_kernel, capacity), out_shape=(jax....]
where the time goes in v2:
time: 115 us
  Pallas kernels  104 us (90%)
  local copies, waits for them, and re-layouts  10.4 us (9%)
    pallas_call x1, Pallas kernels, relay_shards(): pl.pallas_call(functools.partial(relay_kernel, capacity), out_shape=(jax....  104 us
    unnamed x10, local copies, waits for them, and re-layouts  10.4 us

profile of v2, /device:TPU:1, one launch (start us, length us, event | category | flops | bytes accessed | tf_op | source)
XLA Modules:
  0.0 115.0 jit_solution(8221256618222526626)
XLA Ops:
  0.6 104.0 %shard_map.111 = (f32[520,1152]{1,0:T(8,128)}, f32[520,1152]{1,0:T(8,128)}, f32[520,1152]{1,0:T(8,128)}, bf16[520,4608]{1,0:T(8,128)(2,1)}) custom-call(s32[1,8]{1,0:T(1,128)} %counts_ref.1, s32[8,128]{1,0:T(8,128)} %bitcast.7, bf16[8,128,1152]{2,1,0:T(8,128)(2,1)} %bitcast.5, bf16[512,4608]{1,0:T(8,128)(2,1)} %hidden_hbm.1, bf16[520,512]{1,0:T(8,128)(2,1)} %bitcast.6, ...), custom_call_target="tpu_custom_call" | custom-call | tf_op jit(solution)/shard_map/pallas_call | solution.py:662
  104.6 0.0 slice-start
  104.6 3.4 %copy.16 = f32[520,1152]{1,0:T(8,128)} copy(f32[520,1152]{1,0:T(8,128)} %get-tuple-element.8) | data formatting | bytes 4792320
  108.0 0.0 copy-start
  108.0 0.0 slice-start.1
  108.0 3.4 %copy.17 = f32[520,1152]{1,0:T(8,128)} copy(f32[520,1152]{1,0:T(8,128)} %get-tuple-element.9) | data formatting | bytes 4792320
  111.4 0.0 copy-done
  111.4 1.4 %copy.18 = f32[520,1152]{1,0:T(8,128)} copy(f32[520,1152]{1,0:T(8,128)S(1)} %copy-done) | data formatting | bytes 4792320
  112.8 0.0 slice-done
  112.8 0.0 slice-done.1
  112.8 2.2 %copy.19 = bf16[520,4608]{1,0:T(8,128)(2,1)} copy(bf16[520,4608]{1,0:T(8,128)(2,1)S(1)} %bitcast.4) | data formatting | bytes 9584640
  (1 shorter events, 0.0 us)
Async XLA Ops:
  104.6 8.2 %slice-start = ((s8[4792320]{0:T(1024)(128)(4,1)}), s8[4194304]{0:T(1024)(128)(4,1)S(1)}, s32[]{:S(2)}) async-start(s8[4792320]{0:T(1024)(128)(4,1)} %bitcast.3), calls=%async_computation | async-start | bytes 8388608
  108.0 3.4 %copy-start = (f32[520,1152]{1,0:T(8,128)S(1)}, f32[520,1152]{1,0:T(8,128)}, u32[]{:S(2)}) copy-start(f32[520,1152]{1,0:T(8,128)} %get-tuple-element.10) | copy-start | bytes 7188484
  108.0 4.8 %slice-start.1 = ((s8[4792320]{0:T(1024)(128)(4,1)}), s8[598016]{0:T(1024)(128)(4,1)S(1)}, s32[]{:S(2)}) async-start(s8[4792320]{0:T(1024)(128)(4,1)} %bitcast.3), calls=%async_computation.1 | async-start | bytes 1196032
